TPU v7x, 128 devices: a whole 4x4x4 slice. The times are simulated.
128 devices in a mesh: row: 8 (over y, z_lo), col: 16 (over z_hi, x, core).
Axes of the slice: x: 4, y: 4, z: 4 (z_hi: 2, z_lo: 2; z = z_hi * 2 + z_lo), core: 2. Of those that a mesh axis runs over, the one named last changes fastest.
Arguments:
- velocities: bfloat16 [1024, 61440], P(None, 'row'), may hold values from -60 to 60, as said below
- modes_panel: bfloat16 [61440, 4096], P('row', 'col'), may hold values from -1 to 1
- atom_slot: int32 [20480], P('row'), may hold values from 0 to 2559, as said below
- lag_offsets: int32 [8], replicated, may hold values from 0 to 256, as said below
Outputs:
- correlations: float32 [8, 4096, 4096], P(None, 'row', 'col')
Inputs may be any that keep to these rules, and one draw needn't show every extreme that they name: `velocities`: every snapshot row has its own scale. Within each aligned block of 2560 atoms, atom_slot is a permutation of 0 to 2559. `lag_offsets`: one of the lags equals 256.
All inputs are finite; a program needn't handle non-finite values.
Results may differ from a plain program's by a relative error of at most 0.0041.
Values may be sent and summed in bfloat16 or wider, within the bound.
A program may use at most 128 MiB of HBM per device.

v0:
```python
import jax
import jax.numpy as jnp
from jax import lax
from jax.sharding import PartitionSpec as P

M = 4096
LAGS = 8
MAXLAG = 256
epsilon = 1e-06


def reorder(modes_panel, atom_slot):
    per_atom = modes_panel.reshape(atom_slot.shape[0], 3, modes_panel.shape[1])
    return jnp.take(per_atom, atom_slot, axis=0).reshape(modes_panel.shape)


def correlate(row_modes, column_modes, lag_offsets):
    snapshots = column_modes.shape[0]
    padded = jnp.concatenate(
        [column_modes, jnp.zeros((MAXLAG, column_modes.shape[1]), jnp.bfloat16)], axis=0
    )
    results = []
    for number in range(LAGS):
        offset = lag_offsets[number]
        shifted = lax.dynamic_slice_in_dim(padded, offset, snapshots, 0)
        product = lax.dot_general(
            row_modes, shifted, (((0,), (0,)), ((), ())), preferred_element_type=jnp.float32
        )
        results.append(product * lax.rsqrt((snapshots - offset).astype(jnp.float32)))
    return jnp.stack(results)


def local(velocities, modes_panel, atom_slot, lag_offsets):
    panel = reorder(modes_panel, atom_slot)
    row_count = lax.axis_size("row")
    partial_terms = jnp.dot(velocities, panel, preferred_element_type=jnp.float32)
    projected = lax.psum(partial_terms, "row")
    energy = lax.psum(jnp.sum(projected * projected, axis=1), "col")
    column_modes = (projected * lax.rsqrt(energy / M + epsilon)[:, None]).astype(jnp.bfloat16)
    block_width = M // row_count
    every_mode = lax.all_gather(column_modes, "col", axis=1, tiled=True)
    row_modes = lax.dynamic_slice_in_dim(
        every_mode, lax.axis_index("row") * block_width, block_width, 1
    )
    return correlate(row_modes, column_modes, lag_offsets)


def solution(mesh):
    return jax.shard_map(
        local,
        mesh=mesh,
        in_specs=(P(None, "row"), P("row", "col"), P("row"), P()),
        out_specs=P(None, "row", "col"),
        check_vma=False,
    )
```

profile of v0, /device:TPU:1, one launch (start us, length us, event | category | flops | bytes accessed | tf_op | source)
XLA Modules:
  0.0 265.8 jit_solution(16931310440080507958)
XLA Ops:
  6.5 0.0 all-reduce.3.cloned.1.call-start
  6.5 0.7 compare_select_fusion
  7.2 0.7 compare_and_fusion
  8.0 11.0 %reshape.12 = bf16[2560,3,256]{2,1,0:T(4,128)(2,1)} reshape(bf16[7680,256]{1,0:T(8,128)(2,1)} %param.5) | data formatting | bytes 7864320 | tf_op jit(solution)/shard_map/reshape | solution.py:13
  18.9 13.3 %gather_fusion = bf16[2560,3,256]{2,1,0:T(4,128)(2,1)} fusion(bf16[2560,3,256]{2,1,0:T(4,128)(2,1)} %reshape.12, s32[3072]{0:T(1024)S(1)} %pad_clamp_fusion), kind=kCustom, calls=%fused_computation | custom fusion | bytes 7874560 | tf_op jit(solution)/shard_map/jit(_take)/gather | solution.py:14
  32.3 10.7 %gather.7 = bf16[7680,256]{1,0:T(8,128)(2,1)} reshape(bf16[2560,3,256]{2,1,0:T(4,128)(2,1)} %gather_fusion) | data formatting | bytes 7864320 | tf_op jit(solution)/shard_map/jit(_take)/gather | solution.py:14
  42.9 1.3 broadcast_in_dim.18
  44.3 1.1 broadcast_in_dim.19
  45.3 12.0 %fusion.4 = f32[1024,256]{0,1:T(8,128)} fusion(bf16[1024,7680]{1,0:T(8,128)(2,1)} %param.4, bf16[7680,256]{1,0:T(8,128)(2,1)} %gather.7, pred[7680]{0:T(1024)(128)(4,1)S(1)} %broadcast_in_dim.19), kind=kOutput, calls=%fused_computation.5 | convolution fusion | flops 4028497920 | bytes 20717056 | tf_op jit(solution)/shard_map/dot_general | solution.py:36
  57.3 0.0 copy-start.1
  57.3 0.0 all-reduce.3.cloned.1.call-update
  57.3 0.0 all-gather.2.cloned.1.call-start
  57.4 77.0 %all-reduce.3.cloned.1.call-done = f32[1024,256]{0,1:T(8,128)} async-done(((f32[1024,256]{0,1:T(8,128)}), f32[1024,256]{0,1:T(8,128)}) %all-reduce.3.cloned.1.call-update) | async-done | bytes 1048592 | tf_op jit(solution)/shard_map/psum | solution.py:37
  134.4 1.3 multiply_reduce_fusion
  135.7 37.5 %psum.15 = f32[1024]{0:T(1024)S(1)} all-reduce(f32[1024]{0:T(1024)S(1)} %multiply_reduce_fusion), channel_id=1, replica_groups=mesh['row'=8,'col'=16] {'col'}, use_global_device_ids=true, to_apply=%region_2.3 | all-reduce | flops 1024 | bytes 8192 | tf_op jit(solution)/shard_map/psum | solution.py:38
  173.2 2.1 multiply_convert_fusion
  175.3 0.0 all-gather.2.cloned.1.call-update
  175.4 0.0 copy-done.1
  175.4 0.7 fusion.48
  196.7 49.1 %all-gather.2.cloned.1.call-done = bf16[1024,4096]{0,1:T(8,128)(2,1)} async-done(((bf16[1024,256]{0,1:T(8,128)(2,1)}), bf16[1024,4096]{0,1:T(8,128)(2,1)}) %all-gather.2.cloned.1.call-update) | async-done | bytes 8388624 | tf_op jit(solution)/shard_map/all_gather | solution.py:41
  245.8 2.0 fusion.22
  247.9 2.4 fusion.20
  250.2 0.0 copy-done
  250.3 1.8 fusion.18
  252.1 1.8 fusion.16
  253.9 0.0 copy-done.2
  253.9 0.6 fusion.14
  254.4 0.6 fusion.12
  255.0 0.6 fusion.10
  255.6 0.0 copy-start.3
  255.6 2.0 copy-done.3
  257.6 1.4 fusion.8
  (4 shorter events, 0.0 us)
Async XLA Ops:
  6.5 127.8 %all-reduce.3.cloned.1.call-start = ((), (), s32[]{:S(2)}) async-start(), calls=%async_computation | async-start | bytes 2097152 | tf_op jit(solution)/shard_map/psum | solution.py:37
  57.3 118.1 %copy-start.1 = (s32[8]{0:T(128)S(1)}, s32[8]{0:T(128)}, u32[]{:S(2)}) copy-start(s32[8]{0:T(128)} %param.7) | copy-start | bytes 100
  57.3 188.5 %all-gather.2.cloned.1.call-start = ((), (), s32[]{:S(2)}) async-start(), calls=%async_computation.1 | async-start | bytes 8912896 | tf_op jit(solution)/shard_map/all_gather | solution.py:41
  175.3 74.9 %copy-start = (bf16[1024,256]{0,1:T(8,128)(2,1)S(1)}, bf16[1024,256]{0,1:T(8,128)(2,1)}, u32[]{:S(2)}) copy-start(bf16[1024,256]{0,1:T(8,128)(2,1)} %multiply_convert_fusion) | copy-start | bytes 1572868
  245.8 8.0 %copy-start.2 = (bf16[1024,4096]{0,1:T(8,128)(2,1)S(1)}, bf16[1024,4096]{0,1:T(8,128)(2,1)}, u32[]{:S(2)}) copy-start(bf16[1024,4096]{0,1:T(8,128)(2,1)} %all-gather.2.cloned.1.call-done) | copy-start | bytes 25165828
  255.6 2.0 copy-start.3
Sparse Core Ops, SparseCore 0:
  57.5 76.8 all-reduce.2
  175.5 70.2 all-gather.1
where the time goes:
time: 267 us; the launch traced here: 266 us
  waiting for transfers between devices  126 us (47%)
  local copies, waits for them, and re-layouts  40.1 us (15%)
  blocking collectives  37.5 us (14%)
  between operations  34.2 us (13%)
  matrix products  23 us (9%)
  other arithmetic  4.87 us (2%)
    psum x1, waiting for transfers between devices, local(): projected = lax.psum(partial_terms, 'row')  77 us
    all_gather x1, waiting for transfers between devices, local(): every_mode = lax.all_gather(column_modes, 'col', axis=1, tiled=True)  49.1 us
    psum x1, blocking collectives, local(): energy = lax.psum(jnp.sum(projected * projected, axis=1), 'col')  37.5 us
    gather x2, local copies, waits for them, and re-layouts, reorder(): return jnp.take(per_atom, atom_slot, axis=0).reshape(modes_panel.shape)  24 us
    dot_general x1, matrix products, local(): jnp.dot(velocities, panel, preferred_element_type=jnp.float32)  12 us
    dot_general x8, matrix products, correlate(): lax.dot_general(row_modes, shifted, (((0,), (0,)), ((), ())), preferred_e...  11.1 us
    reshape x1, local copies, waits for them, and re-layouts, reorder(): per_atom = modes_panel.reshape(atom_slot.shape[0], 3, modes_panel.shape[1])  11 us
  transfers between devices with their start and end apart: 2, of which 2 were waited for; matrix products, arithmetic and copies ran while one was open for 0% of the time, Pallas kernels for 0%

commit v1 on v0

--- a/solution.py
+++ b/solution.py
@@ -38,7 +38,9 @@
     energy = lax.psum(jnp.sum(projected * projected, axis=1), "col")
     column_modes = (projected * lax.rsqrt(energy / M + epsilon)[:, None]).astype(jnp.bfloat16)
     block_width = M // row_count
-    every_mode = lax.all_gather(column_modes, "col", axis=1, tiled=True)
+    every_mode = jnp.concatenate(
+        lax.all_to_all(jnp.stack([column_modes] * lax.axis_size("col")), "col", 0, 0), axis=1
+    )
     row_modes = lax.dynamic_slice_in_dim(
         every_mode, lax.axis_index("row") * block_width, block_width, 1
     )

time: 267 us -> 322 us (1.21)
  waiting for transfers between devices: 126 us -> 168 us
  starting transfers between devices: 0.04 us -> 5.25 us
  local copies, waits for them, and re-layouts: 40.1 us -> 44.3 us
  matrix products: 23 us -> 27.1 us
    all_to_all x0 -> x1, waiting for transfers between devices: none -> 90.9 us  [local(): lax.all_to_all(jnp.stack([column_modes] * lax.axis_size('col')), 'col', 0...]
    all_gather x1 -> x0, waiting for transfers between devices: 49.1 us -> none  [local(): every_mode = lax.all_gather(column_modes, 'col', axis=1, tiled=True)]
    all_to_all x0 -> x1, starting transfers between devices: none -> 5.24 us  [local(): lax.all_to_all(jnp.stack([column_modes] * lax.axis_size('col')), 'col', 0...]
    another operation x0 -> x1, local copies, waits for them, and re-layouts: none -> 4.29 us  [local(): jnp.stack([column_modes] * lax.axis_size('col'))]
    dot_general x8, matrix products: 11.1 us -> 15.1 us  [correlate(): lax.dot_general(row_modes, shifted, (((0,), (0,)), ((), ())), preferred_e...]
where the time goes in v1:
time: 322 us; the launch traced here: 320 us
  waiting for transfers between devices  168 us (52%)
  local copies, waits for them, and re-layouts  44.3 us (14%)
  blocking collectives  37.3 us (12%)
  between operations  34 us (11%)
  matrix products  27.1 us (8%)
  starting transfers between devices  5.25 us (2%)
  other arithmetic  4.08 us (1%)
    all_to_all x1, waiting for transfers between devices, local(): lax.all_to_all(jnp.stack([column_modes] * lax.axis_size('col')), 'col', 0...  90.9 us
    psum x1, waiting for transfers between devices, local(): projected = lax.psum(partial_terms, 'row')  77.2 us
    psum x1, blocking collectives, local(): energy = lax.psum(jnp.sum(projected * projected, axis=1), 'col')  37.3 us
    gather x2, local copies, waits for them, and re-layouts, reorder(): return jnp.take(per_atom, atom_slot, axis=0).reshape(modes_panel.shape)  24 us
    dot_general x8, matrix products, correlate(): lax.dot_general(row_modes, shifted, (((0,), (0,)), ((), ())), preferred_e...  15.1 us
    dot_general x1, matrix products, local(): jnp.dot(velocities, panel, preferred_element_type=jnp.float32)  12 us
    reshape x1, local copies, waits for them, and re-layouts, reorder(): per_atom = modes_panel.reshape(atom_slot.shape[0], 3, modes_panel.shape[1])  11 us
  transfers between devices with their start and end apart: 2, of which 2 were waited for; matrix products, arithmetic and copies ran while one was open for 0% of the time, Pallas kernels for 0%

profile of v1, /device:TPU:1, one launch (start us, length us, event | category | flops | bytes accessed | tf_op | source)
XLA Modules:
  0.0 320.3 jit_solution(14458628609356651888)
XLA Ops:
  6.5 0.0 all-reduce.3.cloned.1.call-start
  6.5 0.7 compare_select_fusion
  7.2 0.7 compare_and_fusion
  8.0 11.0 %reshape.20 = bf16[2560,3,256]{2,1,0:T(4,128)(2,1)} reshape(bf16[7680,256]{1,0:T(8,128)(2,1)} %param.5) | data formatting | bytes 7864320 | tf_op jit(solution)/shard_map/reshape | solution.py:13
  18.9 13.3 %gather_fusion = bf16[2560,3,256]{2,1,0:T(4,128)(2,1)} fusion(bf16[2560,3,256]{2,1,0:T(4,128)(2,1)} %reshape.20, s32[3072]{0:T(1024)S(1)} %pad_clamp_fusion), kind=kCustom, calls=%fused_computation | custom fusion | bytes 7874560 | tf_op jit(solution)/shard_map/jit(_take)/gather | solution.py:14
  32.3 10.7 %gather.7 = bf16[7680,256]{1,0:T(8,128)(2,1)} reshape(bf16[2560,3,256]{2,1,0:T(4,128)(2,1)} %gather_fusion) | data formatting | bytes 7864320 | tf_op jit(solution)/shard_map/jit(_take)/gather | solution.py:14
  42.9 1.3 broadcast_in_dim.18
  44.3 1.1 broadcast_in_dim.19
  45.3 12.0 %fusion.4 = f32[1024,256]{0,1:T(8,128)} fusion(bf16[1024,7680]{1,0:T(8,128)(2,1)} %param.4, bf16[7680,256]{1,0:T(8,128)(2,1)} %gather.7, pred[7680]{0:T(1024)(128)(4,1)S(1)} %broadcast_in_dim.19), kind=kOutput, calls=%fused_computation.5 | convolution fusion | flops 4028497920 | bytes 20717056 | tf_op jit(solution)/shard_map/dot_general | solution.py:36
  57.3 0.0 all-reduce.3.cloned.1.call-update
  57.3 77.2 %all-reduce.3.cloned.1.call-done = f32[1024,256]{0,1:T(8,128)} async-done(((f32[1024,256]{0,1:T(8,128)}), f32[1024,256]{0,1:T(8,128)}) %all-reduce.3.cloned.1.call-update) | async-done | bytes 1048592 | tf_op jit(solution)/shard_map/psum | solution.py:37
  134.5 1.3 multiply_reduce_fusion
  135.9 37.3 %psum.15 = f32[1024]{0:T(1024)S(1)} all-reduce(f32[1024]{0:T(1024)S(1)} %multiply_reduce_fusion), channel_id=1, replica_groups=mesh['row'=8,'col'=16] {'col'}, use_global_device_ids=true, to_apply=%region_2.3 | all-reduce | flops 1024 | bytes 8192 | tf_op jit(solution)/shard_map/psum | solution.py:38
  173.2 1.3 multiply_convert_fusion
  174.5 4.3 %stack.20 = bf16[16,1024,256]{1,2,0:T(8,128)(2,1)} broadcast(bf16[1024,256]{0,1:T(8,128)(2,1)S(1)} %multiply_convert_fusion), dimensions={1,2} | broadcast | bytes 8912896 | tf_op jit(solution)/shard_map/stack | solution.py:42
  178.8 0.0 copy-start
  178.8 5.2 %all-to-all-start = ((bf16[16,1024,256]{1,2,0:T(8,128)(2,1)}), bf16[16,1024,256]{1,2,0:T(8,128)(2,1)}, u32[]{:S(2)}, u32[]{:S(2)}) async-start(bf16[16,1024,256]{1,2,0:T(8,128)(2,1)} %stack.20), calls=%async_computation | async-start | bytes 16777216 | tf_op jit(solution)/shard_map/all_to_all | solution.py:42
  184.1 0.0 copy-done
  184.1 0.7 fusion.48
  205.3 90.9 %all-to-all-done = bf16[16,1024,256]{1,2,0:T(8,128)(2,1)} async-done(((bf16[16,1024,256]{1,2,0:T(8,128)(2,1)}), bf16[16,1024,256]{1,2,0:T(8,128)(2,1)}, u32[]{:S(2)}, u32[]{:S(2)}) %all-to-all-start) | async-done | bytes 8388640 | tf_op jit(solution)/shard_map/all_to_all | solution.py:42
  296.2 1.8 fusion.22
  298.0 1.8 fusion.20
  299.8 1.8 fusion.18
  301.6 1.8 fusion.16
  303.4 1.8 fusion.14
  305.2 1.8 fusion.12
  307.0 1.8 fusion.10
  308.8 0.0 copy-start.1
  308.8 2.0 copy-done.1
  310.8 2.6 fusion.8
  (2 shorter events, 0.0 us)
Async XLA Ops:
  6.5 128.0 %all-reduce.3.cloned.1.call-start = ((), (), s32[]{:S(2)}) async-start(), calls=%async_computation.1 | async-start | bytes 2097152 | tf_op jit(solution)/shard_map/psum | solution.py:37
  178.8 5.2 %copy-start = (s32[8]{0:T(128)S(1)}, s32[8]{0:T(128)}, u32[]{:S(2)}) copy-start(s32[8]{0:T(128)} %param.7) | copy-start | bytes 100
  178.8 117.4 %all-to-all-start = ((bf16[16,1024,256]{1,2,0:T(8,128)(2,1)}), bf16[16,1024,256]{1,2,0:T(8,128)(2,1)}, u32[]{:S(2)}, u32[]{:S(2)}) async-start(bf16[16,1024,256]{1,2,0:T(8,128)(2,1)} %stack.20), calls=%async_computation | async-start | bytes 16777216 | tf_op jit(solution)/shard_map/all_to_all | solution.py:42
  308.8 2.0 copy-start.1
Sparse Core Ops, SparseCore 0:
  57.5 77.0 all-reduce.2

commit v2 on v0

--- a/solution.py
+++ b/solution.py
@@ -35,7 +35,7 @@
     row_count = lax.axis_size("row")
     partial_terms = jnp.dot(velocities, panel, preferred_element_type=jnp.float32)
     projected = lax.psum(partial_terms, "row")
-    energy = lax.psum(jnp.sum(projected * projected, axis=1), "col")
+    energy = jnp.sum(lax.all_gather(jnp.sum(projected * projected, axis=1), "col"), axis=0)
     column_modes = (projected * lax.rsqrt(energy / M + epsilon)[:, None]).astype(jnp.bfloat16)
     block_width = M // row_count
     every_mode = lax.all_gather(column_modes, "col", axis=1, tiled=True)

time: 267 us -> 256 us (0.959)
  blocking collectives: 37.5 us -> 28.8 us
    psum x1 -> x0, blocking collectives: 37.5 us -> none  [local(): energy = lax.psum(jnp.sum(projected * projected, axis=1), 'col')]
    all_gather x0 -> x1, blocking collectives: none -> 28.8 us  [local(): lax.all_gather(jnp.sum(projected * projected, axis=1), 'col')]
where the time goes in v2:
time: 256 us; the launch traced here: 255 us
  waiting for transfers between devices  124 us (48%)
  local copies, waits for them, and re-layouts  40.1 us (16%)
  between operations  34.2 us (13%)
  blocking collectives  28.8 us (11%)
  matrix products  23 us (9%)
  other arithmetic  4.89 us (2%)
    psum x1, waiting for transfers between devices, local(): projected = lax.psum(partial_terms, 'row')  77 us
    all_gather x1, waiting for transfers between devices, local(): every_mode = lax.all_gather(column_modes, 'col', axis=1, tiled=True)  46.6 us
    all_gather x1, blocking collectives, local(): lax.all_gather(jnp.sum(projected * projected, axis=1), 'col')  28.8 us
    gather x2, local copies, waits for them, and re-layouts, reorder(): return jnp.take(per_atom, atom_slot, axis=0).reshape(modes_panel.shape)  24 us
    dot_general x1, matrix products, local(): jnp.dot(velocities, panel, preferred_element_type=jnp.float32)  12 us
    dot_general x8, matrix products, correlate(): lax.dot_general(row_modes, shifted, (((0,), (0,)), ((), ())), preferred_e...  11.1 us
    reshape x1, local copies, waits for them, and re-layouts, reorder(): per_atom = modes_panel.reshape(atom_slot.shape[0], 3, modes_panel.shape[1])  11 us
  transfers between devices with their start and end apart: 2, of which 2 were waited for; matrix products, arithmetic and copies ran while one was open for 0% of the time, Pallas kernels for 0%

profile of v2, /device:TPU:1, one launch (start us, length us, event | category | flops | bytes accessed | tf_op | source)
XLA Modules:
  0.0 254.6 jit_solution(15133176027254937114)
XLA Ops:
  6.5 0.0 all-reduce.3.cloned.1.call-start
  6.5 0.7 compare_select_fusion
  7.2 0.7 compare_and_fusion
  8.0 11.0 %reshape.16 = bf16[2560,3,256]{2,1,0:T(4,128)(2,1)} reshape(bf16[7680,256]{1,0:T(8,128)(2,1)} %param.5) | data formatting | bytes 7864320 | tf_op jit(solution)/shard_map/reshape | solution.py:13
  18.9 13.3 %gather_fusion = bf16[2560,3,256]{2,1,0:T(4,128)(2,1)} fusion(bf16[2560,3,256]{2,1,0:T(4,128)(2,1)} %reshape.16, s32[3072]{0:T(1024)S(1)} %pad_clamp_fusion), kind=kCustom, calls=%fused_computation | custom fusion | bytes 7874560 | tf_op jit(solution)/shard_map/jit(_take)/gather | solution.py:14
  32.3 10.7 %gather.7 = bf16[7680,256]{1,0:T(8,128)(2,1)} reshape(bf16[2560,3,256]{2,1,0:T(4,128)(2,1)} %gather_fusion) | data formatting | bytes 7864320 | tf_op jit(solution)/shard_map/jit(_take)/gather | solution.py:14
  42.9 1.3 broadcast_in_dim.18
  44.3 1.1 broadcast_in_dim.19
  45.3 12.0 %fusion.4 = f32[1024,256]{0,1:T(8,128)} fusion(bf16[1024,7680]{1,0:T(8,128)(2,1)} %param.4, bf16[7680,256]{1,0:T(8,128)(2,1)} %gather.7, pred[7680]{0:T(1024)(128)(4,1)S(1)} %broadcast_in_dim.19), kind=kOutput, calls=%fused_computation.5 | convolution fusion | flops 4028497920 | bytes 20717056 | tf_op jit(solution)/shard_map/dot_general | solution.py:36
  57.3 0.0 copy-start.1
  57.3 0.0 all-reduce.3.cloned.1.call-update
  57.3 0.0 all-gather.3.cloned.1.call-start
  57.4 77.0 %all-reduce.3.cloned.1.call-done = f32[1024,256]{0,1:T(8,128)} async-done(((f32[1024,256]{0,1:T(8,128)}), f32[1024,256]{0,1:T(8,128)}) %all-reduce.3.cloned.1.call-update) | async-done | bytes 1048592 | tf_op jit(solution)/shard_map/psum | solution.py:37
  134.4 1.3 multiply_reduce_fusion
  135.7 28.8 %all-gather = f32[16384]{0:T(1024)S(1)} all-gather(f32[1024]{0:T(1024)S(1)} %multiply_reduce_fusion), channel_id=2, replica_groups=mesh['row'=8,'col'=16] {'col'}, dimensions={0}, use_global_device_ids=true | all-gather | bytes 69632 | tf_op jit(solution)/shard_map/all_gather | solution.py:38
  164.6 2.1 multiply_convert_fusion
  166.7 0.0 all-gather.3.cloned.1.call-update
  166.8 0.0 copy-done.1
  166.8 0.7 fusion.48
  188.1 46.6 %all-gather.3.cloned.1.call-done = bf16[1024,4096]{0,1:T(8,128)(2,1)} async-done(((bf16[1024,256]{0,1:T(8,128)(2,1)}), bf16[1024,4096]{0,1:T(8,128)(2,1)}) %all-gather.3.cloned.1.call-update) | async-done | bytes 8388624 | tf_op jit(solution)/shard_map/all_gather | solution.py:41
  234.7 2.0 fusion.22
  236.7 2.4 fusion.20
  239.1 0.0 copy-done
  239.1 1.8 fusion.18
  240.9 1.8 fusion.16
  242.7 0.0 copy-done.2
  242.7 0.6 fusion.14
  243.3 0.6 fusion.12
  243.8 0.6 fusion.10
  244.4 0.0 copy-start.3
  244.4 2.0 copy-done.3
  246.4 1.4 fusion.8
  (6 shorter events, 0.0 us)
Async XLA Ops:
  6.5 127.8 %all-reduce.3.cloned.1.call-start = ((), (), s32[]{:S(2)}) async-start(), calls=%async_computation | async-start | bytes 2097152 | tf_op jit(solution)/shard_map/psum | solution.py:37
  57.3 109.4 %copy-start.1 = (s32[8]{0:T(128)S(1)}, s32[8]{0:T(128)}, u32[]{:S(2)}) copy-start(s32[8]{0:T(128)} %param.7) | copy-start | bytes 100
  57.3 177.3 %all-gather.3.cloned.1.call-start = ((), (), s32[]{:S(2)}) async-start(), calls=%async_computation.1 | async-start | bytes 8912896 | tf_op jit(solution)/shard_map/all_gather | solution.py:41
  166.7 72.3 %copy-start = (bf16[1024,256]{0,1:T(8,128)(2,1)S(1)}, bf16[1024,256]{0,1:T(8,128)(2,1)}, u32[]{:S(2)}) copy-start(bf16[1024,256]{0,1:T(8,128)(2,1)} %multiply_convert_fusion) | copy-start | bytes 1572868
  234.7 8.0 %copy-start.2 = (bf16[1024,4096]{0,1:T(8,128)(2,1)S(1)}, bf16[1024,4096]{0,1:T(8,128)(2,1)}, u32[]{:S(2)}) copy-start(bf16[1024,4096]{0,1:T(8,128)(2,1)} %all-gather.3.cloned.1.call-done) | copy-start | bytes 25165828
  244.4 2.0 copy-start.3
Sparse Core Ops, SparseCore 0:
  57.5 76.8 all-reduce.2
  166.9 67.7 all-gather.2
